TPU v7x, 32 devices: a whole 2x2x4 slice. The times are simulated.
32 devices in a mesh: wide: 4 (over x, core), narrow: 8 (over z, y).
Axes of the slice: x: 2, y: 2, z: 4, core: 2. Of those that a mesh axis runs over, the one named last changes fastest.
Arguments:
- basis_t: bfloat16 [2048, 64, 256], P(('wide', 'narrow')), may hold values from -0.375 to 0.375
- nested_transfer_matrices: float32 [64, 64, 4096], P(None, None, ('wide', 'narrow')), may hold values from -0.22 to 0.93
- leaf_coupling: float32 [64, 64, 16384], P(None, None, ('wide', 'narrow')), may hold values from -6 to 6
- leaf_columns: int32 [16384], P(('wide', 'narrow')), may hold values from 0 to 2047, as said below
- far_coupling: float32 [64, 64, 512], P(None, None, ('wide', 'narrow')), may hold values from -6 to 6
- far_columns: int32 [512], P(('wide', 'narrow')), may hold values from 0 to 3, as said below
Outputs:
- leaf_coupled: float32 [64, 64, 16384], P(None, None, ('wide', 'narrow'))
- far_coupled: float32 [64, 64, 512], P(None, None, ('wide', 'narrow'))
- group_factors: float32 [32, 64, 64], P(('wide', 'narrow'))
Inputs may be any that keep to these rules, and one draw needn't show every extreme that they name: `leaf_columns`: block b's column leaf lies 2 to 64 leaves away from its row leaf b // 8; on every device some block lies exactly 64 leaves away. `far_columns`: block f's column branch differs from its row branch f // 128.
All inputs are finite; a program needn't handle non-finite values.
Results may differ from a plain program's by a relative error of at most 0.0003.
Values sent between devices are 32-bit elements; how exact they have to be, the bound alone decides.
A program may use at most 192 MiB of HBM per device.

v0:
```python
import functools

import jax
import jax.numpy as jnp
from jax import lax
from jax.experimental import pallas as pl
from jax.experimental.pallas import tpu as pltpu
from jax.sharding import PartitionSpec as P

F32, BF16 = jnp.float32, jnp.bfloat16
VMEM_LIMIT = 56 * 1024 * 1024
NN = (((1,), (0,)), ((), ()))
NT = (((1,), (1,)), ((), ()))


def mm(a, b, dims):
    return lax.dot_general(a, b, dims, preferred_element_type=F32)


def halves(x):
    high = x.astype(BF16)
    return high, (x - high.astype(F32)).astype(BF16)


def mm3(a, b, dims):
    ah, al = halves(a)
    bh, bl = halves(b)
    return mm(ah, bh, dims) + (mm(al, bh, dims) + mm(ah, bl, dims))


def fold(x):
    h = x.shape[0] // 2
    return jnp.concatenate([x[:h], x[h:]], axis=1)


def unfold(x):
    w = x.shape[1] // 2
    return jnp.concatenate([x[:, :w], x[:, w:]], axis=0)


def cholesky_lanes(work, upper, rank):
    lanes = work.shape[2]
    upper[...] = jnp.zeros_like(upper)
    for c0 in range(0, rank, 8):
        left = rank - c0
        if c0 > 0:
            for first in range(c0, c0 + 8, 4):

                def body(e, acc, c0=c0, first=first):
                    v = upper[e, c0:, :]
                    return tuple(
                        acc[r] - upper[e, first + r : first + r + 1, :] * v for r in range(4)
                    )

                acc = tuple(work[first + r, c0:, :] for r in range(4))
                acc = lax.fori_loop(0, c0, body, acc, unroll=4)
                for r in range(4):
                    work[first + r, c0:, :] = acc[r]
        rows = [work[c0 + r, c0:, :] for r in range(8)]
        ids = lax.broadcasted_iota(jnp.int32, (left, lanes), 0)
        for r in range(8):
            pivot = rows[r][r : r + 1]
            v = rows[r] * (1.0 / jnp.sqrt(pivot))
            v = jnp.where(ids >= r, v, 0.0)
            upper[c0 + r, c0:, :] = v
            for later in range(r + 1, 8):
                rows[later] = rows[later] - v[later : later + 1] * v


def leaf_kernel(basis, folded, stage, work, upper):
    leaves, rank = basis.shape[0], basis.shape[1]
    half = rank // 2

    def gram(t, carry):
        b = basis[t]
        stage[pl.ds(t, half, stride=leaves), :] = fold(mm(b, b, NT))
        return carry

    lax.fori_loop(0, leaves, gram, 0, unroll=4)
    for i in range(half):
        turned = stage[i * leaves : (i + 1) * leaves, :].T
        work[i] = turned[:rank]
        work[i + half] = turned[rank:]
    cholesky_lanes(work, upper, rank)
    for i in range(half):
        both = jnp.concatenate([upper[i], upper[i + half]], axis=0)
        stage[i * leaves : (i + 1) * leaves, :] = both.T

    def put(t, carry):
        folded[t] = stage[pl.ds(t, half, stride=leaves), :]
        return carry

    lax.fori_loop(0, leaves, put, 0, unroll=4)


def climb_kernel(basis, transfer, root, message, turned, grams):
    leaves, rank = basis.shape[0], basis.shape[1]
    half = rank // 2
    slots = transfer.shape[1]

    def turn(i, carry):
        both = jnp.concatenate(
            [
                transfer[pl.ds(i, rank, stride=rank), :],
                transfer[pl.ds(i + half, rank, stride=rank), :],
            ],
            axis=0,
        )
        turned[pl.ds(pl.multiple_of(i * slots, slots), slots), :] = both.T
        return carry

    lax.fori_loop(0, half, turn, 0, unroll=4)

    def table(h):
        return unfold(turned[pl.ds(h, half, stride=slots), :])

    def term(g, f):
        return mm3(mm3(f, g, NN), f, NT)

    count = leaves

    def first(p, carry):
        b0, b1 = basis[2 * p], basis[2 * p + 1]
        grams[p] = term(mm(b0, b0, NT), table(count + 2 * p)) + term(
            mm(b1, b1, NT), table(count + 2 * p + 1)
        )
        return carry

    lax.fori_loop(0, count // 2, first, 0, unroll=4)
    count //= 2
    while count > 1:

        def level(p, carry, count=count):
            grams[p] = term(grams[2 * p], table(count + 2 * p)) + term(
                grams[2 * p + 1], table(count + 2 * p + 1)
            )
            return carry

        lax.fori_loop(0, count // 2, level, 0, unroll=min(4, count // 2))
        count //= 2
    root[...] = grams[0]
    message[...] = jnp.concatenate([term(grams[0], table(1)), table(0)], axis=1)


def branch_kernel(slot, gathered, root, group_upper, branch_upper, nodes, stage, work, upper):
    group, rank = gathered.shape[0], gathered.shape[1]
    half = rank // 2
    nodes[0] = root[...]
    count = group
    terms = [gathered[n][:, :rank] for n in range(group)]
    while count > 1:
        count //= 2
        for p in range(count):
            nodes[count + p] = terms[2 * p] + terms[2 * p + 1]
        if count > 1:
            made = []
            for p in range(count):
                f = gathered[count + p][:, rank:]
                made.append(mm3(mm3(f, nodes[count + p], NN), f, NT))
            terms = made
    stage[...] = jnp.ones_like(stage)
    stage[pl.ds(0, half, stride=8), :] = fold(nodes[slot[0]])
    stage[pl.ds(1, half, stride=8), :] = fold(nodes[1])
    for i in range(half):
        turned = stage[i * 8 : (i + 1) * 8, :].T
        work[i] = turned[:rank]
        work[i + half] = turned[rank:]
    cholesky_lanes(work, upper, rank)
    for i in range(half):
        both = jnp.concatenate([upper[i], upper[i + half]], axis=0)
        stage[i * 8 : (i + 1) * 8, :] = both.T
    group_upper[...] = unfold(stage[pl.ds(0, half, stride=8), :])
    branch_upper[...] = stage[pl.ds(1, half, stride=8), :]


def couple_kernel(per_leaf, tables, cols, own, *refs):
    x, out, ready, turned, mid, done = refs[tables:]
    half = own.shape[1]
    rank = 2 * half
    slab = x.shape[1]
    step = pl.program_id(0)

    @pl.when(step == 0)
    def _():
        for place, ref in enumerate(refs[:tables]):
            leaves = ref.shape[0]

            def prepare(t, carry, first=place * leaves, ref=ref):
                hi, lo = halves(unfold(ref[t]))
                ready[first + t] = jnp.concatenate([hi, hi, lo], axis=1)
                return carry

            lax.fori_loop(0, leaves, prepare, 0, unroll=4)

    def turn(j, carry):
        both = jnp.concatenate(
            [x[pl.ds(j, rank, stride=rank), :], x[pl.ds(j + half, rank, stride=rank), :]], axis=0
        )
        turned[j] = both.T
        return carry

    lax.fori_loop(0, half, turn, 0, unroll=4)
    here = slab // per_leaf

    def leaf(t, carry):
        rows = turned[:, pl.ds(pl.multiple_of(t * per_leaf, per_leaf), per_leaf), :]
        a = rows.reshape(half * per_leaf, 2 * rank)
        ah, al = halves(a)
        u = unfold(own[step * here + t])
        zero = jnp.zeros_like(u)
        wide = jnp.concatenate(
            [jnp.concatenate([u, zero], axis=1), jnp.concatenate([zero, u], axis=1)], axis=0
        )
        wh, wl = halves(wide)
        mid[...] = mm(
            jnp.concatenate([ah, al], axis=1), jnp.concatenate([wh, wh], axis=1), NT
        ) + mm(ah, wl, NT)
        for n in range(per_leaf):
            h = unfold(mid[pl.ds(n, half, stride=per_leaf), :])
            hh, hl = halves(h)
            s = cols[step * slab + t * per_leaf + n]
            made = mm(ready[s], jnp.concatenate([hh, hl, hh], axis=0), NN)
            done[pl.ds(t * per_leaf + n, half, stride=slab), :] = fold(made)
        return carry

    lax.fori_loop(0, here, leaf, 0, unroll=2)

    def turn_back(l, carry):
        back = done[pl.ds(pl.multiple_of(l * slab, slab), slab), :].T
        out[pl.ds(l, rank, stride=rank), :] = back[:rank]
        out[pl.ds(l + half, rank, stride=rank), :] = back[rank:]
        return carry

    lax.fori_loop(0, half, turn_back, 0, unroll=4)


def vmem():
    return pl.BlockSpec(memory_space=pltpu.VMEM)


def smem():
    return pl.BlockSpec(memory_space=pltpu.SMEM)


def params():
    return pltpu.CompilerParams(vmem_limit_bytes=VMEM_LIMIT)


def leaf_factors(basis_t):
    leaves, rank = basis_t.shape[:2]
    half = rank // 2
    return pl.pallas_call(
        leaf_kernel,
        out_shape=jax.ShapeDtypeStruct((leaves, half, 2 * rank), F32),
        in_specs=[vmem()],
        out_specs=vmem(),
        scratch_shapes=[
            pltpu.VMEM((half * leaves, 2 * rank), F32),
            pltpu.VMEM((rank, rank, leaves), F32),
            pltpu.VMEM((rank, rank, leaves), F32),
        ],
        compiler_params=params(),
        name="leaf_factors",
    )(basis_t)


def climb(basis_t, transfer):
    leaves, rank = basis_t.shape[:2]
    slots = transfer.shape[2]
    return pl.pallas_call(
        climb_kernel,
        out_shape=(
            jax.ShapeDtypeStruct((rank, rank), F32),
            jax.ShapeDtypeStruct((rank, 2 * rank), F32),
        ),
        in_specs=[vmem(), vmem()],
        out_specs=(vmem(), vmem()),
        scratch_shapes=[
            pltpu.VMEM((rank // 2 * slots, 2 * rank), F32),
            pltpu.VMEM((leaves // 2, rank, rank), F32),
        ],
        compiler_params=params(),
        name="climb",
    )(basis_t, transfer.reshape(rank * rank, slots))


def branch(slot, gathered, root):
    group, rank = gathered.shape[:2]
    return pl.pallas_call(
        branch_kernel,
        out_shape=(
            jax.ShapeDtypeStruct((rank, rank), F32),
            jax.ShapeDtypeStruct((rank // 2, 2 * rank), F32),
        ),
        in_specs=[smem(), vmem(), vmem()],
        out_specs=(vmem(), vmem()),
        scratch_shapes=[
            pltpu.VMEM((group, rank, rank), F32),
            pltpu.VMEM((rank // 2 * 8, 2 * rank), F32),
            pltpu.VMEM((rank, rank, 8), F32),
            pltpu.VMEM((rank, rank, 8), F32),
        ],
        compiler_params=params(),
        name="branch",
    )(slot, gathered, root)


def couple(cols, own, tables, coupling):
    leaves, half = own.shape[:2]
    kept = tables[0].shape[0]
    rank = 2 * half
    blocks = coupling.shape[2]
    slab = min(128, blocks)
    per_leaf = blocks // leaves
    out = pl.pallas_call(
        functools.partial(couple_kernel, per_leaf, len(tables)),
        out_shape=jax.ShapeDtypeStruct((rank * rank, blocks), F32),
        grid=(blocks // slab,),
        in_specs=[
            smem(),
            *[pl.BlockSpec(f.shape, lambda g: (0, 0, 0)) for f in (own, *tables)],
            pl.BlockSpec((rank * rank, slab), lambda g: (0, g)),
        ],
        out_specs=pl.BlockSpec((rank * rank, slab), lambda g: (0, g)),
        scratch_shapes=[
            pltpu.VMEM((len(tables) * kept, rank, 3 * rank), BF16),
            pltpu.VMEM((half, slab, 2 * rank), F32),
            pltpu.VMEM((half * per_leaf, 2 * rank), F32),
            pltpu.VMEM((half * slab, 2 * rank), F32),
        ],
        compiler_params=params(),
        name="couple",
    )(cols, own, *tables, coupling.reshape(rank * rank, blocks))
    return out.reshape(rank, rank, blocks)


def on_device(
    basis_t, nested_transfer_matrices, leaf_coupling, leaf_columns, far_coupling, far_columns
):
    leaves = basis_t.shape[0]
    both = ("wide", "narrow")
    devices = lax.axis_size(both)
    first_leaf = lax.axis_index(both) * leaves - leaves
    own = leaf_factors(basis_t)
    before = lax.ppermute(own, both, [(i, i + 1) for i in range(devices - 1)])
    after = lax.ppermute(own, both, [(i + 1, i) for i in range(devices - 1)])
    root, message = climb(basis_t, nested_transfer_matrices)
    gathered = lax.all_gather(message, "narrow", axis=0)
    leaf_coupled = couple(leaf_columns - first_leaf, own, (before, own, after), leaf_coupling)

    group = lax.axis_size("narrow")
    depth = group.bit_length() - 1
    n = lax.axis_index("narrow")
    slot = jnp.zeros((), jnp.int32)
    for level in range(1, depth + 1):
        slot = jnp.where(n % 2**level == 2 ** (level - 1) - 1, (group + n) >> level, slot)
    group_upper, branch_upper = branch(slot.reshape(1).astype(jnp.int32), gathered, root)
    branch_all = lax.all_gather(branch_upper, "wide", axis=0)
    far_coupled = couple(far_columns, branch_upper[None], (branch_all,), far_coupling)
    return (leaf_coupled, far_coupled, group_upper[None])


def solution(mesh):
    in_specs = (
        P(("wide", "narrow"), None, None),
        P(None, None, ("wide", "narrow")),
        P(None, None, ("wide", "narrow")),
        P(("wide", "narrow")),
        P(None, None, ("wide", "narrow")),
        P(("wide", "narrow")),
    )
    out_specs = (
        P(None, None, ("wide", "narrow")),
        P(None, None, ("wide", "narrow")),
        P(("wide", "narrow"), None, None),
    )
    return jax.shard_map(
        on_device, mesh=mesh, in_specs=in_specs, out_specs=out_specs, check_vma=False
    )
```

profile of v0, /device:TPU:0, one launch (start us, length us, event | category | flops | bytes accessed | tf_op | source)
XLA Modules:
  0.0 183.4 jit_solution(12503367668418884149)
XLA Ops:
  0.6 11.7 %leaf_factors.1.own.refs_1_ = f32[64,32,128]{2,1,0:T(8,128)} custom-call(bf16[64,64,256]{2,1,0:T(8,128)(2,1)} %basis.3), custom_call_target="tpu_custom_call" | custom-call | tf_op jit(solution)/shard_map/leaf_factors/pallas_call | solution.py:252
  12.4 1.3 collective-permute-start.1
  13.7 5.6 %collective-permute-start = (f32[64,32,128]{2,1,0:T(8,128)}, f32[64,32,128]{2,1,0:T(8,128)S(1)}, u32[]{:S(2)}, u32[]{:S(2)}) collective-permute-start(f32[64,32,128]{2,1,0:T(8,128)} %leaf_factors.1.own.refs_1_), channel_id=1, source_target_pairs={{0,1},{1,2},{2,3},{3,4},{4,5},{5,6},{6,7},{7,8},{8,9},{9,10},{10,1... | collective-permute-start | bytes 3145736 | tf_op jit(solution)/shard_map/ppermute | solution.py:345
  19.3 0.0 copy-start.2
  19.3 29.2 %climb.1 = (f32[64,64]{1,0:T(8,128)}, f32[64,128]{1,0:T(8,128)}) custom-call(bf16[64,64,256]{2,1,0:T(8,128)(2,1)} %basis.3, f32[4096,128]{1,0:T(8,128)} %bitcast.14), custom_call_target="tpu_custom_call" | custom-call | tf_op jit(solution)/shard_map/climb/pallas_call | solution.py:270
  48.5 0.0 copy-done.2
  48.5 0.0 copy-start.3
  48.5 1.9 %copy.9 = f32[64,64,16]{2,1,0:T(8,128)} copy(f32[64,64,16]{1,2,0:T(8,128)S(1)} %copy-done.2) | data formatting | bytes 524288 | tf_op args[4]
  50.4 0.0 copy-done.3
  50.4 41.4 %all-gather = f32[512,128]{1,0:T(8,128)} all-gather(f32[64,128]{1,0:T(8,128)S(1)} %copy-done.3), channel_id=2, replica_groups=mesh['wide'=4,'narrow'=8] {'narrow'}, dimensions={0}, use_global_device_ids=true | all-gather | bytes 294912 | tf_op jit(solution)/shard_map/all_gather | solution.py:348
  91.8 7.0 %branch.1 = (f32[64,64]{1,0:T(8,128)}, f32[32,128]{1,0:T(8,128)}) custom-call(s32[1]{0:T(128)} %bitcast.2.slot, f32[8,64,128]{2,1,0:T(8,128)} %bitcast.15, f32[64,64]{1,0:T(8,128)} %get-tuple-element.8.root), custom_call_target="tpu_custom_call" | custom-call | tf_op jit(solution)/shard_map/branch/pallas_call | solution.py:289
  98.8 5.9 %all-gather.1 = f32[128,128]{1,0:T(8,128)} all-gather(f32[32,128]{1,0:T(8,128)} %get-tuple-element.9), channel_id=3, replica_groups=mesh['wide'=4,'narrow'=8] {'wide'}, dimensions={0}, use_global_device_ids=true | all-gather | bytes 81920 | tf_op jit(solution)/shard_map/all_gather | solution.py:358
  104.7 7.6 %couple.3 = f32[4096,16]{1,0:T(8,128)} custom-call(s32[16]{0:T(128)} %cols.1, f32[1,32,128]{2,1,0:T(8,128)} %bitcast.17, f32[4,32,128]{2,1,0:T(8,128)} %bitcast.16, f32[4096,16]{1,0:T(8,128)} %bitcast.10), custom_call_target="tpu_custom_call" | custom-call | tf_op jit(solution)/shard_map/couple/pallas_call | solution.py:315
  112.3 0.0 copy-start.4
  112.3 3.0 %copy.10 = f32[64,64,16]{1,2,0:T(8,128)} copy(f32[64,64,16]{2,1,0:T(8,128)} %bitcast.11) | data formatting | bytes 524288
  115.3 0.0 copy-done.4
  115.3 0.5 broadcast_subtract_fusion.cols
  115.8 0.0 collective-permute-done.1.refs_2_
  115.8 0.0 copy-start
  115.8 0.0 collective-permute-done.refs_0_
  115.8 0.0 copy-start.1
  115.9 1.0 copy-done
  116.9 0.3 copy-done.1
  117.2 66.2 %couple.2 = f32[4096,512]{1,0:T(8,128)} custom-call(s32[512]{0:T(512)} %broadcast_subtract_fusion.cols, f32[64,32,128]{2,1,0:T(8,128)} %leaf_factors.1.own.refs_1_, f32[64,32,128]{2,1,0:T(8,128)} %copy-done.1, f32[64,32,128]{2,1,0:T(8,128)} %leaf_factors.1.own.refs_1_, f32[64,32,128]{2,1,0:T(8,128)} %copy-done, f32[4096,512]{1,0:T(8,128)} %bitcast.12), custom_call_target="tpu_custom_call" | custom-call | tf_op jit(solution)/shard_map/couple/pallas_call | solution.py:315
Async XLA Ops:
  12.4 103.5 %collective-permute-start.1 = (f32[64,32,128]{2,1,0:T(8,128)}, f32[64,32,128]{2,1,0:T(8,128)S(1)}, u32[]{:S(2)}, u32[]{:S(2)}) collective-permute-start(f32[64,32,128]{2,1,0:T(8,128)} %leaf_factors.1.own.refs_1_), channel_id=1, source_target_pairs={{1,0},{2,1},{3,2},{4,3},{5,4},{6,5},{7,6},{8,7},{9,8},{10,9},{11,1... | collective-permute-start | bytes 3145736 | tf_op jit(solution)/shard_map/ppermute | solution.py:346
  13.7 102.2 %collective-permute-start = (f32[64,32,128]{2,1,0:T(8,128)}, f32[64,32,128]{2,1,0:T(8,128)S(1)}, u32[]{:S(2)}, u32[]{:S(2)}) collective-permute-start(f32[64,32,128]{2,1,0:T(8,128)} %leaf_factors.1.own.refs_1_), channel_id=1, source_target_pairs={{0,1},{1,2},{2,3},{3,4},{4,5},{5,6},{6,7},{7,8},{8,9},{9,10},{10,1... | collective-permute-start | bytes 3145736 | tf_op jit(solution)/shard_map/ppermute | solution.py:345
  19.3 29.2 %copy-start.2 = (f32[64,64,16]{1,2,0:T(8,128)S(1)}, f32[64,64,16]{1,2,0:T(8,128)}, u32[]{:S(2)}) copy-start(f32[64,64,16]{1,2,0:T(8,128)} %param.10) | copy-start | bytes 786436
  48.5 1.9 %copy-start.3 = (f32[64,128]{1,0:T(8,128)S(1)}, f32[64,128]{1,0:T(8,128)}, u32[]{:S(2)}) copy-start(f32[64,128]{1,0:T(8,128)} %get-tuple-element.7) | copy-start | bytes 98308
  112.3 3.0 %copy-start.4 = (s32[512]{0:T(512)S(1)}, s32[512]{0:T(512)}, u32[]{:S(2)}) copy-start(s32[512]{0:T(512)} %param.9) | copy-start | bytes 6148
  115.8 1.0 copy-start
  115.8 1.3 copy-start.1
where the time goes:
time: 184 us; the launch traced here: 183 us
  Pallas kernels  122 us (66%)
  blocking collectives  47.3 us (26%)
  starting transfers between devices  6.84 us (4%)
  local copies, waits for them, and re-layouts  6.25 us (3%)
    pallas_call x2, Pallas kernels, couple(): pl.pallas_call(functools.partial(couple_kernel, per_leaf, len(tables)), o...  73.8 us
    all_gather x1, blocking collectives, on_device(): gathered = lax.all_gather(message, 'narrow', axis=0)  41.4 us
    pallas_call x1, Pallas kernels, climb(): pl.pallas_call(climb_kernel, out_shape=(jax.ShapeDtypeStruct((rank, rank)...  29.2 us
    pallas_call x1, Pallas kernels, leaf_factors(): pl.pallas_call(leaf_kernel, out_shape=jax.ShapeDtypeStruct((leaves, half,...  11.7 us
    pallas_call x1, Pallas kernels, branch(): pl.pallas_call(branch_kernel, out_shape=(jax.ShapeDtypeStruct((rank, rank...  7.04 us
    unnamed x12, local copies, waits for them, and re-layouts  6.25 us
    all_gather x1, blocking collectives, on_device(): branch_all = lax.all_gather(branch_upper, 'wide', axis=0)  5.89 us
    ppermute x1, starting transfers between devices, on_device(): before = lax.ppermute(own, both, [(i, i + 1) for i in range(devices - 1)])  5.56 us
  transfers between devices with their start and end apart: 2, of which 0 were waited for; matrix products, arithmetic and copies ran while one was open for 3% of the time, Pallas kernels for 24%

commit v1 on v0

--- a/solution.py
+++ b/solution.py
@@ -126,7 +126,7 @@
         )
         return carry
 
-    lax.fori_loop(0, count // 2, first, 0, unroll=4)
+    lax.fori_loop(0, count // 2, first, 0, unroll=16)
     count //= 2
     while count > 1:
 
@@ -136,7 +136,7 @@
             )
             return carry
 
-        lax.fori_loop(0, count // 2, level, 0, unroll=min(4, count // 2))
+        lax.fori_loop(0, count // 2, level, 0, unroll=min(16, count // 2))
         count //= 2
     root[...] = grams[0]
     message[...] = jnp.concatenate([term(grams[0], table(1)), table(0)], axis=1)
@@ -202,28 +202,32 @@
     lax.fori_loop(0, half, turn, 0, unroll=4)
     here = slab // per_leaf
 
-    def leaf(t, carry):
-        rows = turned[:, pl.ds(pl.multiple_of(t * per_leaf, per_leaf), per_leaf), :]
-        a = rows.reshape(half * per_leaf, 2 * rank)
-        ah, al = halves(a)
-        u = unfold(own[step * here + t])
-        zero = jnp.zeros_like(u)
-        wide = jnp.concatenate(
-            [jnp.concatenate([u, zero], axis=1), jnp.concatenate([zero, u], axis=1)], axis=0
-        )
-        wh, wl = halves(wide)
-        mid[...] = mm(
-            jnp.concatenate([ah, al], axis=1), jnp.concatenate([wh, wh], axis=1), NT
-        ) + mm(ah, wl, NT)
-        for n in range(per_leaf):
-            h = unfold(mid[pl.ds(n, half, stride=per_leaf), :])
-            hh, hl = halves(h)
-            s = cols[step * slab + t * per_leaf + n]
-            made = mm(ready[s], jnp.concatenate([hh, hl, hh], axis=0), NN)
-            done[pl.ds(t * per_leaf + n, half, stride=slab), :] = fold(made)
-        return carry
-
-    lax.fori_loop(0, here, leaf, 0, unroll=2)
+    together = mid.shape[0]
+
+    def some(first, carry):
+        for m in range(together):
+            t = first * together + m
+            rows = turned[:, pl.ds(pl.multiple_of(t * per_leaf, per_leaf), per_leaf), :]
+            ah, al = halves(rows.reshape(half * per_leaf, 2 * rank))
+            u = unfold(own[step * here + t])
+            zero = jnp.zeros_like(u)
+            wide = jnp.concatenate(
+                [jnp.concatenate([u, zero], axis=1), jnp.concatenate([zero, u], axis=1)], axis=0
+            )
+            wh, wl = halves(wide)
+            mid[m] = mm(
+                jnp.concatenate([ah, al], axis=1), jnp.concatenate([wh, wh], axis=1), NT
+            ) + mm(ah, wl, NT)
+        for m in range(together):
+            for n in range(per_leaf):
+                b = (first * together + m) * per_leaf + n
+                hh, hl = halves(unfold(mid[m, pl.ds(n, half, stride=per_leaf), :]))
+                s = cols[step * slab + b]
+                made = mm(ready[s], jnp.concatenate([hh, hl, hh], axis=0), NN)
+                done[pl.ds(b, half, stride=slab), :] = fold(made)
+        return carry
+
+    lax.fori_loop(0, here // together, some, 0)
 
     def turn_back(l, carry):
         back = done[pl.ds(pl.multiple_of(l * slab, slab), slab), :].T
@@ -232,6 +236,53 @@
         return carry
 
     lax.fori_loop(0, half, turn_back, 0, unroll=4)
+
+
+def spread_kernel(axis, x, out, send, recv, local):
+    count = out.shape[0]
+    me = lax.axis_index(axis)
+    barrier = pltpu.get_barrier_semaphore()
+    for k in range(1, count):
+        pl.semaphore_signal(
+            barrier,
+            inc=1,
+            device_id={axis: lax.rem(me + k, count)},
+            device_id_type=pl.DeviceIdType.MESH,
+        )
+    pl.semaphore_wait(barrier, count - 1)
+    copies = [pltpu.make_async_copy(x, out.at[me], local)]
+    for k in range(1, count):
+        copies.append(
+            pltpu.make_async_remote_copy(
+                src_ref=x,
+                dst_ref=out.at[me],
+                send_sem=send.at[k - 1],
+                recv_sem=recv.at[k - 1],
+                device_id={axis: lax.rem(me + k, count)},
+                device_id_type=pl.DeviceIdType.MESH,
+            )
+        )
+    for copy in copies:
+        copy.start()
+    for copy in copies:
+        copy.wait()
+
+
+def spread(x, axis, collective_id):
+    count = lax.axis_size(axis)
+    return pl.pallas_call(
+        functools.partial(spread_kernel, axis),
+        out_shape=jax.ShapeDtypeStruct((count,) + x.shape, x.dtype),
+        in_specs=[vmem()],
+        out_specs=vmem(),
+        scratch_shapes=[
+            pltpu.SemaphoreType.DMA((count - 1,)),
+            pltpu.SemaphoreType.DMA((count - 1,)),
+            pltpu.SemaphoreType.DMA,
+        ],
+        compiler_params=pltpu.CompilerParams(collective_id=collective_id, has_side_effects=True),
+        name="spread_" + axis,
+    )(x)
 
 
 def vmem():
@@ -312,6 +363,7 @@
     blocks = coupling.shape[2]
     slab = min(128, blocks)
     per_leaf = blocks // leaves
+    together = min(4, slab // per_leaf)
     out = pl.pallas_call(
         functools.partial(couple_kernel, per_leaf, len(tables)),
         out_shape=jax.ShapeDtypeStruct((rank * rank, blocks), F32),
@@ -325,7 +377,7 @@
         scratch_shapes=[
             pltpu.VMEM((len(tables) * kept, rank, 3 * rank), BF16),
             pltpu.VMEM((half, slab, 2 * rank), F32),
-            pltpu.VMEM((half * per_leaf, 2 * rank), F32),
+            pltpu.VMEM((together, half * per_leaf, 2 * rank), F32),
             pltpu.VMEM((half * slab, 2 * rank), F32),
         ],
         compiler_params=params(),
@@ -345,7 +397,7 @@
     before = lax.ppermute(own, both, [(i, i + 1) for i in range(devices - 1)])
     after = lax.ppermute(own, both, [(i + 1, i) for i in range(devices - 1)])
     root, message = climb(basis_t, nested_transfer_matrices)
-    gathered = lax.all_gather(message, "narrow", axis=0)
+    gathered = spread(message, "narrow", 0)
     leaf_coupled = couple(leaf_columns - first_leaf, own, (before, own, after), leaf_coupling)
 
     group = lax.axis_size("narrow")
@@ -355,7 +407,7 @@
     for level in range(1, depth + 1):
         slot = jnp.where(n % 2**level == 2 ** (level - 1) - 1, (group + n) >> level, slot)
     group_upper, branch_upper = branch(slot.reshape(1).astype(jnp.int32), gathered, root)
-    branch_all = lax.all_gather(branch_upper, "wide", axis=0)
+    branch_all = spread(branch_upper, "wide", 1)
     far_coupled = couple(far_columns, branch_upper[None], (branch_all,), far_coupling)
     return (leaf_coupled, far_coupled, group_upper[None])
 

time: 184 us -> 144 us (0.78)
  blocking collectives: 47.3 us -> 0 us
  Pallas kernels: 122 us -> 127 us
    all_gather x2 -> x0, blocking collectives: 47.3 us -> none  [the longest x1 41.4 us: on_device(): gathered = lax.all_gather(message, 'narrow', axis=0)]
    pallas_call x0 -> x2, Pallas kernels: none -> 30.3 us  [spread(): pl.pallas_call(functools.partial(spread_kernel, axis), out_shape=jax.Shap...]
    pallas_call x2, Pallas kernels: 73.8 us -> 56.2 us  [couple(): pl.pallas_call(functools.partial(couple_kernel, per_leaf, len(tables)), o...]
    pallas_call x1, Pallas kernels: 29.2 us -> 22.1 us  [climb(): pl.pallas_call(climb_kernel, out_shape=(jax.ShapeDtypeStruct((rank, rank)...]
    unnamed x12 -> x10, local copies, waits for them, and re-layouts: 6.25 us -> 6.26 us
  transfers between devices with their start and end apart: 2 -> 2, of which waited for: 0 -> 0; matrix products, arithmetic and copies ran while one was open for 3% -> 4% of each run, Pallas kernels for 24% -> 47%
where the time goes in v1:
time: 144 us; the launch traced here: 142 us
  Pallas kernels  127 us (88%)
  starting transfers between devices  7.03 us (5%)
  local copies, waits for them, and re-layouts  6.26 us (4%)
    pallas_call x2, Pallas kernels, couple(): pl.pallas_call(functools.partial(couple_kernel, per_leaf, len(tables)), o...  56.2 us
    pallas_call x2, Pallas kernels, spread(): pl.pallas_call(functools.partial(spread_kernel, axis), out_shape=jax.Shap...  30.3 us
    pallas_call x1, Pallas kernels, climb(): pl.pallas_call(climb_kernel, out_shape=(jax.ShapeDtypeStruct((rank, rank)...  22.1 us
    pallas_call x1, Pallas kernels, leaf_factors(): pl.pallas_call(leaf_kernel, out_shape=jax.ShapeDtypeStruct((leaves, half,...  11.7 us
    pallas_call x1, Pallas kernels, branch(): pl.pallas_call(branch_kernel, out_shape=(jax.ShapeDtypeStruct((rank, rank...  7.04 us
    unnamed x10, local copies, waits for them, and re-layouts  6.26 us
    ppermute x1, starting transfers between devices, on_device(): before = lax.ppermute(own, both, [(i, i + 1) for i in range(devices - 1)])  5.75 us
  transfers between devices with their start and end apart: 2, of which 0 were waited for; matrix products, arithmetic and copies ran while one was open for 4% of the time, Pallas kernels for 47%

profile of v1, /device:TPU:0, one launch (start us, length us, event | category | flops | bytes accessed | tf_op | source)
XLA Modules:
  0.0 142.0 jit_solution(12974791215162201260)
XLA Ops:
  0.6 11.7 %leaf_factors.1.own.refs_1_ = f32[64,32,128]{2,1,0:T(8,128)} custom-call(bf16[64,64,256]{2,1,0:T(8,128)(2,1)} %basis.3), custom_call_target="tpu_custom_call" | custom-call | tf_op jit(solution)/shard_map/leaf_factors/pallas_call | solution.py:303
  12.4 1.3 collective-permute-start.1
  13.7 5.7 %collective-permute-start = (f32[64,32,128]{2,1,0:T(8,128)}, f32[64,32,128]{2,1,0:T(8,128)S(1)}, u32[]{:S(2)}, u32[]{:S(2)}) collective-permute-start(f32[64,32,128]{2,1,0:T(8,128)} %leaf_factors.1.own.refs_1_), channel_id=1, source_target_pairs={{0,1},{1,2},{2,3},{3,4},{4,5},{5,6},{6,7},{7,8},{8,9},{9,10},{10,1... | collective-permute-start | bytes 3145736 | tf_op jit(solution)/shard_map/ppermute | solution.py:397
  19.4 0.0 copy-start.2
  19.5 22.1 %climb.1 = (f32[64,64]{1,0:T(8,128)}, f32[64,128]{1,0:T(8,128)}) custom-call(bf16[64,64,256]{2,1,0:T(8,128)(2,1)} %basis.3, f32[4096,128]{1,0:T(8,128)} %bitcast.12), custom_call_target="tpu_custom_call" | custom-call | tf_op jit(solution)/shard_map/climb/pallas_call | solution.py:321
  41.6 25.2 %spread_narrow.1.gathered = f32[8,64,128]{2,1,0:T(8,128)} custom-call(f32[64,128]{1,0:T(8,128)} %get-tuple-element.7.x), custom_call_target="tpu_custom_call" | custom-call | tf_op jit(solution)/shard_map/spread_narrow/pallas_call | solution.py:273
  66.8 7.0 %branch.1 = (f32[64,64]{1,0:T(8,128)}, f32[32,128]{1,0:T(8,128)}) custom-call(s32[1]{0:T(128)} %bitcast.2.slot, f32[8,64,128]{2,1,0:T(8,128)} %spread_narrow.1.gathered, f32[64,64]{1,0:T(8,128)} %get-tuple-element.8.root), custom_call_target="tpu_custom_call" | custom-call | tf_op jit(solution)/shard_map/branch/pallas_call | solution.py:340
  73.8 5.1 %spread_wide.1.refs_0_ = f32[4,32,128]{2,1,0:T(8,128)} custom-call(f32[32,128]{1,0:T(8,128)} %get-tuple-element.9.x), custom_call_target="tpu_custom_call" | custom-call | tf_op jit(solution)/shard_map/spread_wide/pallas_call | solution.py:273
  79.0 0.0 copy-done.2
  79.0 1.9 %copy.9 = f32[64,64,16]{2,1,0:T(8,128)} copy(f32[64,64,16]{1,2,0:T(8,128)S(1)} %copy-done.2) | data formatting | bytes 524288 | tf_op args[4]
  80.9 7.6 %couple.3 = f32[4096,16]{1,0:T(8,128)} custom-call(s32[16]{0:T(128)} %cols.1, f32[1,32,128]{2,1,0:T(8,128)} %bitcast.13, f32[4,32,128]{2,1,0:T(8,128)} %spread_wide.1.refs_0_, f32[4096,16]{1,0:T(8,128)} %bitcast.9), custom_call_target="tpu_custom_call" | custom-call | tf_op jit(solution)/shard_map/couple/pallas_call | solution.py:367
  88.5 0.0 copy-start.3
  88.5 3.0 %copy.10 = f32[64,64,16]{1,2,0:T(8,128)} copy(f32[64,64,16]{2,1,0:T(8,128)} %bitcast.8) | data formatting | bytes 524288
  91.5 0.0 copy-done.3
  91.5 0.5 broadcast_subtract_fusion.cols
  92.1 0.0 collective-permute-done.1.refs_2_
  92.1 0.0 copy-start
  92.1 0.0 collective-permute-done.refs_0_
  92.1 0.0 copy-start.1
  92.1 1.0 copy-done
  93.1 0.3 copy-done.1
  93.4 48.6 %couple.2 = f32[4096,512]{1,0:T(8,128)} custom-call(s32[512]{0:T(512)} %broadcast_subtract_fusion.cols, f32[64,32,128]{2,1,0:T(8,128)} %leaf_factors.1.own.refs_1_, f32[64,32,128]{2,1,0:T(8,128)} %copy-done.1, f32[64,32,128]{2,1,0:T(8,128)} %leaf_factors.1.own.refs_1_, f32[64,32,128]{2,1,0:T(8,128)} %copy-done, f32[4096,512]{1,0:T(8,128)} %bitcast.10), custom_call_target="tpu_custom_call" | custom-call | tf_op jit(solution)/shard_map/couple/pallas_call | solution.py:367
Async XLA Ops:
  12.4 79.7 %collective-permute-start.1 = (f32[64,32,128]{2,1,0:T(8,128)}, f32[64,32,128]{2,1,0:T(8,128)S(1)}, u32[]{:S(2)}, u32[]{:S(2)}) collective-permute-start(f32[64,32,128]{2,1,0:T(8,128)} %leaf_factors.1.own.refs_1_), channel_id=1, source_target_pairs={{1,0},{2,1},{3,2},{4,3},{5,4},{6,5},{7,6},{8,7},{9,8},{10,9},{11,1... | collective-permute-start | bytes 3145736 | tf_op jit(solution)/shard_map/ppermute | solution.py:398
  13.7 78.4 %collective-permute-start = (f32[64,32,128]{2,1,0:T(8,128)}, f32[64,32,128]{2,1,0:T(8,128)S(1)}, u32[]{:S(2)}, u32[]{:S(2)}) collective-permute-start(f32[64,32,128]{2,1,0:T(8,128)} %leaf_factors.1.own.refs_1_), channel_id=1, source_target_pairs={{0,1},{1,2},{2,3},{3,4},{4,5},{5,6},{6,7},{7,8},{8,9},{9,10},{10,1... | collective-permute-start | bytes 3145736 | tf_op jit(solution)/shard_map/ppermute | solution.py:397
  19.4 59.5 %copy-start.2 = (f32[64,64,16]{1,2,0:T(8,128)S(1)}, f32[64,64,16]{1,2,0:T(8,128)}, u32[]{:S(2)}) copy-start(f32[64,64,16]{1,2,0:T(8,128)} %param.10) | copy-start | bytes 786436
  88.5 3.0 %copy-start.3 = (s32[512]{0:T(512)S(1)}, s32[512]{0:T(512)}, u32[]{:S(2)}) copy-start(s32[512]{0:T(512)} %param.9) | copy-start | bytes 6148
  92.1 1.0 copy-start
  92.1 1.3 copy-start.1
